TPU v7x, 32 devices: a whole 2x2x4 slice. The times are simulated.
32 devices in a mesh: ex: 4 (over y, x), tp: 4 (over z), ps: 2 (over core).
Axes of the slice: x: 2, y: 2, z: 4, core: 2. Of those that a mesh axis runs over, the one named last changes fastest.
Arguments:
- tokens: bfloat16 [1024, 8192], P(('ex', 'ps'), 'tp'), may hold values from -6 to 6
- output_gradient: bfloat16 [1024, 29568], P(('ex', 'ps'), 'tp'), may hold values from -6 to 6
- adapter_down_factor: bfloat16 [8192, 128], P('tp'), may hold values from -0.0625 to 0.0625
- adapter_up_factor: bfloat16 [29568, 128], P('tp'), may hold values from -0.03125 to 0.03125
- first_moment_down: float32 [4, 2048, 128], P('tp', ('ex', 'ps')), may hold values from -0.012 to 0.012
- second_moment_down: float32 [4, 2048, 128], P('tp', ('ex', 'ps')), may hold values from 2e-07 to 2e-06
- first_moment_up: float32 [4, 7392, 128], P('tp', ('ex', 'ps')), may hold values from -0.012 to 0.012
- second_moment_up: float32 [4, 7392, 128], P('tp', ('ex', 'ps')), may hold values from 2e-07 to 2e-06
- down_row_seeds: int32 [4, 2048], P('tp', ('ex', 'ps')), may hold values from 0 to 15
- up_row_seeds: int32 [4, 7392], P('tp', ('ex', 'ps')), may hold values from 0 to 15
- segments: int32 [1024], replicated, may hold values from 0 to 3, never falling along the last dimension, each value on 1 to 512 neighbouring positions
- bank: bfloat16 [16, 128, 8192], P(None, None, ('ex', 'tp', 'ps')), may hold values from -6 to 6
Outputs:
- sketch: float32 [4, 8192], P(None, ('ex', 'tp', 'ps'))
Inputs may be any that keep to these rules, and one draw needn't show every extreme that they name: `segments`: never falls along the rows; every example has 1 to 512 rows and one has exactly 512.
All inputs are finite; a program needn't handle non-finite values.
Results may differ from a plain program's by a relative error of at most 0.0033.
Values may be sent and summed in bfloat16 or wider, within the bound.
A program may use at most 64 MiB of HBM per device.

v0:
```python
import math

import jax
import jax.numpy as jnp
from jax import lax
from jax.sharding import PartitionSpec as P

MODEL_WIDTH = 8192
HIDDEN_WIDTH = 29568
ADAPTER_RANK = 128
BANK = 16
EXAMPLES = 4


def spread_rows(values, labels):
    count = values.shape[0]
    picks = (labels[:, None] == jnp.arange(EXAMPLES, dtype=jnp.int32)[None, :]).astype(values.dtype)
    return (values[:, None, :] * picks[:, :, None]).reshape(count, EXAMPLES * values.shape[1])


def contract_rows(left, right):
    return lax.dot_general(
        left, right, (((0,), (0,)), ((), ())), preferred_element_type=jnp.float32
    )


def adam_feature(grad, first, second, lengths):
    rows = grad.shape[0]
    scaled_grad = grad.reshape(rows, EXAMPLES, ADAPTER_RANK) / lengths[None, :, None]
    moved = 0.9 * first[0][:, None, :] + 0.1 * scaled_grad
    scaled = 0.999 * second[0][:, None, :] + 0.001 * scaled_grad * scaled_grad
    return moved / (jnp.sqrt(scaled) + 1e-08)


def block_sums(feature, seeds):
    select = (seeds[0][:, None] == jnp.arange(BANK, dtype=jnp.int32)[None, :]).astype(jnp.float32)
    return jnp.einsum("nj,ner->ejr", select, feature, precision=lax.Precision.HIGHEST)


def on_device(
    tokens,
    output_gradient,
    adapter_down_factor,
    adapter_up_factor,
    first_moment_down,
    second_moment_down,
    first_moment_up,
    second_moment_up,
    down_row_seeds,
    up_row_seeds,
    segments,
    bank,
):
    hidden_portion = jnp.dot(tokens, adapter_down_factor, preferred_element_type=jnp.float32)
    input_portion = jnp.dot(output_gradient, adapter_up_factor, preferred_element_type=jnp.float32)
    summed_h, summed_u = lax.psum((hidden_portion, input_portion), "tp")
    hidden_inner_product = summed_h.astype(jnp.bfloat16)
    input_inner_product = summed_u.astype(jnp.bfloat16)
    labels = jnp.arange(EXAMPLES, dtype=jnp.int32)
    lengths = jnp.sum((segments[None, :] == labels[:, None]).astype(jnp.int32), axis=1).astype(
        jnp.float32
    )
    cols_x, cols_g = (
        lax.all_to_all(tokens, ("ex", "ps"), split_axis=1, concat_axis=0, tiled=True),
        lax.all_to_all(output_gradient, ("ex", "ps"), split_axis=1, concat_axis=0, tiled=True),
    )
    piece_h = lax.all_gather(hidden_inner_product, ("ex", "ps"), axis=0, tiled=True)
    piece_u = lax.all_gather(input_inner_product, ("ex", "ps"), axis=0, tiled=True)
    new_a = contract_rows(cols_x, spread_rows(piece_u, segments))
    new_b = contract_rows(cols_g, spread_rows(piece_h, segments))
    feature_a = adam_feature(new_a, first_moment_down, second_moment_down, lengths)
    feature_b = adam_feature(new_b, first_moment_up, second_moment_up, lengths)
    partial_value = block_sums(feature_a, down_row_seeds) + block_sums(feature_b, up_row_seeds)
    summed = lax.psum(partial_value, ("ex", "tp", "ps"))
    inverse = 1.0 / math.sqrt((MODEL_WIDTH + HIDDEN_WIDTH) * ADAPTER_RANK)
    sketch = jnp.einsum(
        "ejr,jrk->ek", summed, bank.astype(jnp.float32), precision=lax.Precision.HIGHEST
    )
    return sketch * inverse


def solution(mesh):
    return jax.shard_map(
        on_device,
        mesh=mesh,
        in_specs=(
            P(("ex", "ps"), "tp"),
            P(("ex", "ps"), "tp"),
            P("tp", None),
            P("tp", None),
            P("tp", ("ex", "ps"), None),
            P("tp", ("ex", "ps"), None),
            P("tp", ("ex", "ps"), None),
            P("tp", ("ex", "ps"), None),
            P("tp", ("ex", "ps")),
            P("tp", ("ex", "ps")),
            P(),
            P(None, None, ("ex", "tp", "ps")),
        ),
        out_specs=P(None, ("ex", "tp", "ps")),
        check_vma=False,
    )
```

profile of v0, /device:TPU:0, one launch (start us, length us, event | category | flops | bytes accessed | tf_op | source)
XLA Modules:
  0.0 122.4 jit_solution(13118332075978798457)
XLA Ops:
  0.0 2.2 %copy.24 = bf16[128,2048]{0,1:T(8,128)(2,1)} copy(bf16[128,2048]{1,0:T(8,128)(2,1)} %param.12) | data formatting | bytes 1048576 | tf_op args[0]
  2.2 5.2 %all-to-all-start = ((bf16[128,8,256]{0,2,1:T(8,128)(2,1)}), bf16[128,8,256]{0,2,1:T(8,128)(2,1)S(1)}, u32[]{:S(2)}, u32[]{:S(2)}) async-start(bf16[128,8,256]{0,2,1:T(8,128)(2,1)} %bitcast.1), calls=%async_computation | async-start | bytes 1048576 | tf_op jit(solution)/shard_map/all_to_all | solution.py:64
  7.4 2.7 %all_to_all.32 = bf16[128,8,924]{0,2,1:T(8,128)(2,1)} reshape(bf16[128,7392]{0,1:T(8,128)(2,1)} %param.13) | data formatting | bytes 3784704 | tf_op jit(solution)/shard_map/all_to_all | solution.py:65
  10.4 2.3 %fusion.44 = f32[128,128]{1,0:T(8,128)S(1)} fusion(bf16[128,7392]{0,1:T(8,128)(2,1)} %param.13, bf16[7392,128]{1,0:T(8,128)(2,1)S(1)} %copy-done), kind=kOutput, calls=%fused_computation.60 | convolution fusion | flops 242221056 | bytes 3850240 | tf_op jit(solution)/shard_map/dot_general | solution.py:55
  12.8 0.9 fusion.24
  13.7 0.7 multiply_bitcast_fusion
  14.5 2.6 %all-to-all-done = bf16[128,8,256]{0,2,1:T(8,128)(2,1)S(1)} async-done(((bf16[128,8,256]{0,2,1:T(8,128)(2,1)}), bf16[128,8,256]{0,2,1:T(8,128)(2,1)S(1)}, u32[]{:S(2)}, u32[]{:S(2)}) %all-to-all-start) | async-done | bytes 524320 | tf_op jit(solution)/shard_map/all_to_all | solution.py:64
  17.1 4.3 %all-to-all-start.1 = ((bf16[128,8,924]{0,2,1:T(8,128)(2,1)}), bf16[128,8,924]{0,2,1:T(8,128)(2,1)}, u32[]{:S(2)}, u32[]{:S(2)}) async-start(bf16[128,8,924]{0,2,1:T(8,128)(2,1)} %all_to_all.32), calls=%async_computation.1 | async-start | bytes 3801088 | tf_op jit(solution)/shard_map/all_to_all | solution.py:65
  21.4 22.0 %all-reduce.2 = (bf16[128,128]{1,0:T(8,128)(2,1)S(1)}, bf16[128,128]{1,0:T(8,128)(2,1)}) all-reduce(f32[128,128]{1,0:T(8,128)S(1)} %fusion.45, f32[128,128]{1,0:T(8,128)S(1)} %fusion.44), channel_id=1, replica_groups=mesh['ex'=4,'tp'=4,'ps'=2] {'tp'}, use_global_device_ids=true, to_apply=%region_2.0 | all-reduce | flops 32768 | bytes 196608 | tf_op jit(solution)/shard_map/psum | solution.py:56
  43.5 9.6 %all_gather.6 = bf16[1024,128]{1,0:T(8,128)(2,1)S(1)} all-gather(bf16[128,128]{1,0:T(8,128)(2,1)} %get-tuple-element.6), channel_id=1, replica_groups=mesh['ex'=4,'tp'=4,'ps'=2] {'ex','ps'}, dimensions={0}, use_global_device_ids=true | all-gather | bytes 294912 | tf_op jit(solution)/shard_map/all_gather | solution.py:68
  53.1 9.1 %all_gather.7 = bf16[1024,128]{1,0:T(8,128)(2,1)S(1)} all-gather(bf16[128,128]{1,0:T(8,128)(2,1)S(1)} %get-tuple-element.5), channel_id=1, replica_groups=mesh['ex'=4,'tp'=4,'ps'=2] {'ex','ps'}, dimensions={0}, use_global_device_ids=true | all-gather | bytes 294912 | tf_op jit(solution)/shard_map/all_gather | solution.py:67
  63.1 1.0 copy_bitcast_fusion.1
  64.2 2.9 %broadcast_multiply_fusion.1 = (bf16[1024,4,128]{2,1,0:T(4,128)(2,1)}, bf16[1024,4,128]{2,1,0:T(4,128)(2,1)S(1)}) fusion(bf16[1024,4]{1,0:T(8,128)(2,1)S(1)} %copy-done.3, bf16[1024,128]{1,0:T(8,128)(2,1)S(1)} %all_gather.6, bf16[1024,128]{1,0:T(8,128)(2,1)S(1)} %all_gather.7), kind=kLoop, calls=%fused_computation.30 | loop fusion | flops 1048576 | bytes 2629632 | tf_op jit(solution)/shard_map/mul | solution.py:18
  67.1 1.0 copy.25
  68.2 1.8 %fusion.10 = f32[512,256]{1,0:T(8,128)S(1)} fusion(bf16[1024,256]{1,0:T(8,128)(2,1)} %bitcast.61, bf16[128,8,4,128]{3,2,1,0:T(4,128)(2,1)} %bitcast.60), kind=kOutput, calls=%fused_computation.15 | convolution fusion | flops 268435456 | bytes 2097152 | tf_op jit(solution)/shard_map/dot_general | solution.py:22
  70.0 1.0 copy.26
  71.0 2.3 %copy.52 = bf16[8,128,924]{1,0,2:T(8,128)(2,1)S(1)} copy(bf16[8,128,924]{1,2,0:T(8,128)(2,1)} %bitcast.9) | data formatting | bytes 3784704 | tf_op jit(solution)/shard_map/all_to_all | solution.py:65
  73.4 0.6 copy.34
  74.0 2.4 %convolution_bitcast_fusion = f32[924,512]{1,0:T(8,128)} fusion(bf16[1024,924]{0,1:T(8,128)(2,1)S(1)} %bitcast.58, bf16[128,8,4,128]{3,2,1,0:T(4,128)(2,1)S(1)} %bitcast.59), kind=kOutput, calls=%fused_computation.8 | convolution fusion | flops 968884224 | bytes 4833280 | tf_op jit(solution)/shard_map/dot_general | solution.py:22
  76.4 2.9 %reshape.105 = f32[924,4,128]{2,1,0:T(4,128)} reshape(f32[924,512]{1,0:T(8,128)} %convolution_bitcast_fusion) | data formatting | bytes 3784704 | tf_op jit(solution)/shard_map/reshape | solution.py:29
  79.4 3.4 %fusion.4 = f32[4,128,16]{1,2,0:T(8,128)S(1)} fusion(f32[924,4,128]{2,1,0:T(4,128)} %reshape.105, f32[924,128]{1,0:T(8,128)S(1)} %copy-done.6, f32[4]{0:T(128)S(1)} %convert_element_type.30, f32[924,128]{1,0:T(8,128)S(1)} %copy-done.7, s32[924]{0:T(1024)S(1)} %bitcast.63), kind=kOutput, calls=%fused_computation.6 | convolution fusion | flops 94632384 | bytes 2875008 | tf_op jit(solution)/shard_map/nj,ner->ejr/dot_general | solution.py:37
  82.9 0.6 fusion.6
  83.5 37.8 %psum.23 = f32[4,16,128]{2,1,0:T(8,128)S(1)} all-reduce(f32[4,16,128]{2,1,0:T(8,128)S(1)} %fusion.6), channel_id=1, replica_groups=mesh['ex'=4,'tp'=4,'ps'=2] {'ex','tp','ps'}, use_global_device_ids=true, to_apply=%region_3.0 | all-reduce | flops 8192 | bytes 65536 | tf_op jit(solution)/shard_map/psum | solution.py:74
  121.3 1.1 fusion.7
  (41 shorter events, 1.6 us)
Async XLA Ops:
  0.0 10.4 %copy-start = (bf16[7392,128]{1,0:T(8,128)(2,1)S(1)}, bf16[7392,128]{1,0:T(8,128)(2,1)}, u32[]{:S(2)}) copy-start(bf16[7392,128]{1,0:T(8,128)(2,1)} %param.15) | copy-start | bytes 5677060
  2.2 14.9 %all-to-all-start = ((bf16[128,8,256]{0,2,1:T(8,128)(2,1)}), bf16[128,8,256]{0,2,1:T(8,128)(2,1)S(1)}, u32[]{:S(2)}, u32[]{:S(2)}) async-start(bf16[128,8,256]{0,2,1:T(8,128)(2,1)} %bitcast.1), calls=%async_computation | async-start | bytes 1048576 | tf_op jit(solution)/shard_map/all_to_all | solution.py:64
  7.4 2.7 %copy-start.1 = (bf16[128,2048]{1,0:T(8,128)(2,1)S(1)}, bf16[128,2048]{1,0:T(8,128)(2,1)}, u32[]{:S(2)}) copy-start(bf16[128,2048]{1,0:T(8,128)(2,1)} %param.12) | copy-start | bytes 1572868
  7.4 2.7 %copy-start.4 = (bf16[2048,128]{1,0:T(8,128)(2,1)S(1)}, bf16[2048,128]{1,0:T(8,128)(2,1)}, u32[]{:S(2)}) copy-start(bf16[2048,128]{1,0:T(8,128)(2,1)} %param.14) | copy-start | bytes 1572868
  10.4 2.3 %copy-start.14 = (s32[1024]{0:T(1024)S(1)}, s32[1024]{0:T(1024)}, u32[]{:S(2)}) copy-start(s32[1024]{0:T(1024)} %param.22) | copy-start | bytes 12292
  10.4 3.3 %copy-start.10 = (f32[1,256,128]{2,1,0:T(8,128)S(1)}, f32[1,256,128]{2,1,0:T(8,128)}, u32[]{:S(2)}) copy-start(f32[1,256,128]{2,1,0:T(8,128)} %param.17) | copy-start | bytes 393220
  10.4 3.3 %copy-start.11 = (f32[1,256,128]{2,1,0:T(8,128)S(1)}, f32[1,256,128]{2,1,0:T(8,128)}, u32[]{:S(2)}) copy-start(f32[1,256,128]{2,1,0:T(8,128)} %param.16) | copy-start | bytes 393220
  14.5 47.7 %copy-start.8 = (f32[1,924,128]{2,0,1:T(1,128)S(1)}, f32[1,924,128]{2,0,1:T(1,128)}, u32[]{:S(2)}) copy-start(f32[1,924,128]{2,0,1:T(1,128)} %param.19) | copy-start | bytes 1419268
  14.5 48.2 %copy-start.9 = (f32[1,924,128]{2,0,1:T(1,128)S(1)}, f32[1,924,128]{2,0,1:T(1,128)}, u32[]{:S(2)}) copy-start(f32[1,924,128]{2,0,1:T(1,128)} %param.18) | copy-start | bytes 1419268
  17.1 53.9 %all-to-all-start.1 = ((bf16[128,8,924]{0,2,1:T(8,128)(2,1)}), bf16[128,8,924]{0,2,1:T(8,128)(2,1)}, u32[]{:S(2)}, u32[]{:S(2)}) async-start(bf16[128,8,924]{0,2,1:T(8,128)(2,1)} %all_to_all.32), calls=%async_computation.1 | async-start | bytes 3801088 | tf_op jit(solution)/shard_map/all_to_all | solution.py:65
  62.1 2.0 %copy-start.3 = (bf16[1024,4]{1,0:T(8,128)(2,1)S(1)}, bf16[1024,4]{1,0:T(8,128)(2,1)}, u32[]{:S(2)}) copy-start(bf16[1024,4]{1,0:T(8,128)(2,1)} %fusion.24) | copy-start | bytes 24580
  76.4 2.9 %copy-start.6 = (f32[924,128]{1,0:T(8,128)S(1)}, f32[924,128]{1,0:T(8,128)}, u32[]{:S(2)}) copy-start(f32[924,128]{1,0:T(8,128)} %get-tuple-element.9) | copy-start | bytes 1419268
  76.4 2.9 %copy-start.7 = (f32[924,128]{1,0:T(8,128)S(1)}, f32[924,128]{1,0:T(8,128)}, u32[]{:S(2)}) copy-start(f32[924,128]{1,0:T(8,128)} %get-tuple-element.10) | copy-start | bytes 1419268
  76.4 2.9 %copy-start.15 = (s32[1,924]{1,0:T(1,128)S(1)}, s32[1,924]{1,0:T(1,128)}, u32[]{:S(2)}) copy-start(s32[1,924]{1,0:T(1,128)} %param.21) | copy-start | bytes 11092
  79.3 3.5 %copy-start.5 = (f32[256,4,128]{2,0,1:T(8,128)S(1)}, f32[256,4,128]{2,0,1:T(8,128)}, u32[]{:S(2)}) copy-start(f32[256,4,128]{2,0,1:T(8,128)} %copy.26) | copy-start | bytes 1572868
  79.3 3.5 %copy-start.12 = (f32[256,128]{1,0:T(8,128)S(1)}, f32[256,128]{1,0:T(8,128)}, u32[]{:S(2)}) copy-start(f32[256,128]{1,0:T(8,128)} %get-tuple-element.11) | copy-start | bytes 393220
  79.3 3.5 %copy-start.13 = (f32[256,128]{1,0:T(8,128)S(1)}, f32[256,128]{1,0:T(8,128)}, u32[]{:S(2)}) copy-start(f32[256,128]{1,0:T(8,128)} %get-tuple-element.12) | copy-start | bytes 393220
  79.3 3.5 %copy-start.16 = (s32[1,256]{1,0:T(1,128)S(1)}, s32[1,256]{1,0:T(1,128)}, u32[]{:S(2)}) copy-start(s32[1,256]{1,0:T(1,128)} %param.20) | copy-start | bytes 3076
  82.8 38.4 %copy-start.2 = (bf16[16,128,256]{2,1,0:T(8,128)(2,1)S(1)}, bf16[16,128,256]{2,1,0:T(8,128)(2,1)}, u32[]{:S(2)}) copy-start(bf16[16,128,256]{2,1,0:T(8,128)(2,1)} %param.23) | copy-start | bytes 3145732
where the time goes:
time: 123 us; the launch traced here: 122 us
  blocking collectives  78.5 us (64%)
  local copies, waits for them, and re-layouts  13.9 us (11%)
  matrix products  12 us (10%)
  starting transfers between devices  9.49 us (8%)
  other arithmetic  5.67 us (5%)
  waiting for transfers between devices  2.63 us (2%)
    psum x1, blocking collectives, on_device(): summed = lax.psum(partial_value, ('ex', 'tp', 'ps'))  37.8 us
    psum x1, blocking collectives, on_device(): summed_h, summed_u = lax.psum((hidden_portion, input_portion), 'tp')  22 us
    all_gather x1, blocking collectives, on_device(): lax.all_gather(input_inner_product, ('ex', 'ps'), axis=0, tiled=True)  9.6 us
    all_gather x1, blocking collectives, on_device(): lax.all_gather(hidden_inner_product, ('ex', 'ps'), axis=0, tiled=True)  9.07 us
    all_to_all x1, starting transfers between devices, on_device(): lax.all_to_all(tokens, ('ex', 'ps'), split_axis=1, concat_axis=0, tiled=T...  5.17 us
    all_to_all x2, local copies, waits for them, and re-layouts, on_device(): lax.all_to_all(output_gradient, ('ex', 'ps'), split_axis=1, concat_axis=0...  4.97 us
    all_to_all x1, starting transfers between devices, on_device(): lax.all_to_all(output_gradient, ('ex', 'ps'), split_axis=1, concat_axis=0...  4.32 us
    dot_general x2, matrix products, contract_rows(): lax.dot_general(left, right, (((0,), (0,)), ((), ())), preferred_element_...  4.26 us
  transfers between devices with their start and end apart: 2, of which 1 were waited for; matrix products, arithmetic and copies ran while one was open for 11% of the time, Pallas kernels for 0%

commit v1 on v0

v1 whole, which is shorter than its diff:
```python
import functools
import math

import jax
import jax.numpy as jnp
from jax import lax
from jax.experimental import pallas as pl
from jax.experimental.pallas import tpu as pltpu
from jax.sharding import PartitionSpec as P

EXAMPLES = 4
BANK = 16
MESH = pl.DeviceIdType.MESH
F32 = jnp.float32
BF16 = jnp.bfloat16


def flip(index, mask):
    out, bit = index, 1
    while bit <= mask:
        if mask & bit:
            out = out + bit - 2 * bit * ((index // bit) % 2)
        bit *= 2
    return out


def up_to(value, step):
    return -(-value // step) * step


def contract_rows(left, right):
    return lax.dot_general(left, right, (((0,), (0,)), ((), ())), preferred_element_type=F32)


def split(value, parts):
    out = []
    for _ in range(parts):
        piece = value.astype(BF16)
        out.append(piece)
        value = value - piece.astype(F32)
    return out


def kernel(
    n_ps, n_plane, n_tp, inverse,
    x_hbm, g_hbm, down_hbm, up_hbm, m1a_hbm, m2a_hbm, m1b_hbm, m2b_hbm, seeds_a, seeds_b, segments, bank_hbm,
    out_ref,
    x, g, down, up, m1a, m2a, m1b, m2b, bank,
    stage, recv, part, part_in, rank_sum, ranks, segcol, acc,
    sums, sums_in, mine, mine_in, total_in, total,
    load_sem, a2a_send, a2a_recv, rs_send, rs_recv, ag_send, ag_recv, pl_send, pl_recv,
    s1_send, s1_recv, s2_send, s2_recv, s3_send, s3_recv,
):
    ex, tp, ps = lax.axis_index("ex"), lax.axis_index("tp"), lax.axis_index("ps")
    q = ex * n_ps + ps
    chip, core = q // 2, q % 2
    n_chip = n_plane // 2
    rows = x.shape[0]
    ra, rb = m1a.shape[1], m1b.shape[1]
    pa = up_to(ra, 128)

    pairs = [(x_hbm, x), (g_hbm, g), (down_hbm, down), (up_hbm, up), (m1a_hbm, m1a), (m2a_hbm, m2a),
             (m1b_hbm, m1b), (m2b_hbm, m2b), (bank_hbm, bank)]
    loads = [pltpu.make_async_copy(a, b, load_sem.at[i]) for i, (a, b) in enumerate(pairs)]
    for load in loads:
        load.start()

    def plane_id(peer):
        return {"ex": peer // n_ps, "ps": peer % n_ps}

    def tp_id(d):
        return {"tp": (tp + d) % n_tp}

    peers = [(mask, other) for mask in range(n_chip) for other in range(2) if mask or other]

    def peer_of(mask, other):
        return 2 * flip(chip, mask) + (core + other) % 2

    barrier = pltpu.get_barrier_semaphore()
    for mask, other in peers:
        pl.semaphore_signal(barrier, inc=1, device_id=plane_id(peer_of(mask, other)), device_id_type=MESH)
    for d in range(1, n_tp):
        pl.semaphore_signal(barrier, inc=1, device_id=tp_id(d), device_id_type=MESH)

    loads[0].wait()
    loads[1].wait()
    for j in range(n_plane):
        stage[j, :, 0:ra] = x[:, j * ra:(j + 1) * ra]
        stage[j, :, pa:pa + rb] = g[:, j * rb:(j + 1) * rb]
    pl.semaphore_wait(barrier, n_plane - 1 + n_tp - 1)

    def plane_copies(src, dst, send, recv_sem, chosen):
        return [
            pltpu.make_async_remote_copy(
                src_ref=src(peer_of(mask, other)), dst_ref=dst, send_sem=send.at[mask, other],
                recv_sem=recv_sem.at[mask, other], device_id=plane_id(peer_of(mask, other)), device_id_type=MESH,
            )
            for mask, other in chosen
        ]

    a2a = plane_copies(lambda peer: stage.at[peer], recv.at[q], a2a_send, a2a_recv, peers)
    late = 2 * max(1, n_chip // 4)
    for copy in a2a[:-late]:
        copy.start()
    recv[q] = stage[q]

    loads[2].wait()
    loads[3].wait()
    part[:, 0:128] = jnp.dot(x[...], down[...], preferred_element_type=F32)
    part[:, 128:256] = jnp.dot(g[...], up[...], preferred_element_type=F32)
    slab = rows // n_tp

    def slab_at(t):
        return pl.ds(pl.multiple_of(t * slab, slab), slab)

    rs = [
        pltpu.make_async_remote_copy(
            src_ref=part.at[slab_at((tp + d) % n_tp)], dst_ref=part_in.at[d - 1], send_sem=rs_send.at[d - 1],
            recv_sem=rs_recv.at[d - 1], device_id=tp_id(d), device_id_type=MESH,
        )
        for d in range(1, n_tp)
    ]
    for copy in rs:
        copy.start()

    seg = segments[...]
    inv_len = [1.0 / jnp.sum((seg == e).astype(F32), axis=(0, 1), keepdims=True) for e in range(EXAMPLES)]
    seg_t = jnp.transpose(seg.astype(F32))
    for j in range(n_plane):
        segcol[j] = jnp.broadcast_to(seg_t[:, j:j + 1], (rows, 128))

    for copy in rs:
        copy.wait()
    summed = part[slab_at(tp), :]
    for d in range(1, n_tp):
        summed = summed + part_in[d - 1]
    rank_sum[...] = summed.astype(BF16)
    ranks[q, slab_at(tp), :] = rank_sum[...]
    ag = [
        pltpu.make_async_remote_copy(
            src_ref=rank_sum, dst_ref=ranks.at[q, slab_at(tp)], send_sem=ag_send.at[d - 1],
            recv_sem=ag_recv.at[d - 1], device_id=tp_id(d), device_id_type=MESH,
        )
        for d in range(1, n_tp)
    ]
    for copy in ag:
        copy.start()
    for copy in ag:
        copy.wait()
    gather = plane_copies(lambda peer: ranks.at[q], ranks.at[q], pl_send, pl_recv, peers)
    for copy in gather:
        copy.start()
    for copy in a2a[-late:]:
        copy.start()

    step = 256
    width = stage.shape[2]
    for mask in range(n_chip):
        for i, (m, _) in enumerate(peers):
            if m == mask:
                gather[i].wait()
                a2a[i].wait()
        first = 2 * flip(chip, mask)
        both = ranks[pl.ds(first, 2)].reshape(2 * rows, 256).astype(F32)
        labels = segcol[pl.ds(first, 2)].reshape(2 * rows, 128)
        picked_h = jnp.concatenate([jnp.where(labels == e, both[:, 0:128], 0.0) for e in range(EXAMPLES)], 1).astype(BF16)
        picked_u = jnp.concatenate([jnp.where(labels == e, both[:, 128:256], 0.0) for e in range(EXAMPLES)], 1).astype(BF16)
        spans = [(s, min(s + step, pa), picked_u) for s in range(0, pa, step)]
        spans += [(s, min(s + step, width), picked_h) for s in range(pa, width, step)]
        for lo, hi, picked in spans:
            block = recv[pl.ds(first, 2), :, lo:hi].reshape(2 * rows, hi - lo)
            term = contract_rows(block, picked)
            if mask == 0:
                acc[lo:hi, :] = term
            else:
                acc[lo:hi, :] += term

    for load in loads[4:]:
        load.wait()
    bins = lax.broadcasted_iota(jnp.int32, (BANK, 128), 0)
    summed = [jnp.zeros((BANK, 128), F32) for _ in range(EXAMPLES)]
    for base, count, m1, m2, seeds in ((0, ra, m1a, m2a, seeds_a), (pa, rb, m1b, m2b, seeds_b)):
        for lo in range(0, count, 128):
            size = min(128, count - lo)
            first = 0.9 * m1[0, lo:lo + size, :]
            second = 0.999 * m2[0, lo:lo + size, :]
            select = (seeds[:, lo:lo + size] == bins[:, :size]).astype(BF16)
            for e in range(EXAMPLES):
                grad = acc[base + lo:base + lo + size, e * 128:(e + 1) * 128] * inv_len[e]
                moved = first + 0.1 * grad
                scaled = second + 0.001 * grad * grad
                feature = moved / (jnp.sqrt(scaled) + 1e-08)
                for piece in split(feature, 2):
                    summed[e] = summed[e] + jnp.dot(select, piece, preferred_element_type=F32)

    share = sums.shape[1]
    every = jnp.concatenate(summed, axis=0)
    for j in range(n_plane):
        sums[j] = every[j * share:(j + 1) * share, :]
    scatter = plane_copies(lambda peer: sums.at[peer], sums_in.at[q], s1_send, s1_recv, peers)
    for copy in scatter:
        copy.start()
    sums_in[q] = sums[q]
    for copy in scatter:
        copy.wait()
    mine[...] = jnp.sum(sums_in[...], axis=0)
    cross = [
        pltpu.make_async_remote_copy(
            src_ref=mine, dst_ref=mine_in.at[tp], send_sem=s2_send.at[d - 1], recv_sem=s2_recv.at[d - 1],
            device_id=tp_id(d), device_id_type=MESH,
        )
        for d in range(1, n_tp)
    ]
    for copy in cross:
        copy.start()
    mine_in[tp] = mine[...]
    for copy in cross:
        copy.wait()
    total_in[q] = jnp.sum(mine_in[...], axis=0)
    spread = plane_copies(lambda peer: total_in.at[q], total_in.at[q], s3_send, s3_recv, peers)
    for copy in spread:
        copy.start()
    for copy in spread:
        copy.wait()
    for j in range(n_plane):
        total[j * share:(j + 1) * share, :] = total_in[j]

    flat = jnp.concatenate([total[pl.ds(j, EXAMPLES, stride=BANK), :] for j in range(BANK)], axis=1)
    bank_rows = bank[...].reshape(BANK * 128, bank.shape[2])
    result = jnp.zeros(out_ref.shape, F32)
    for piece in split(flat, 3):
        result = result + jnp.dot(piece, bank_rows, preferred_element_type=F32)
    out_ref[...] = result * inverse


def on_device(n_ps, n_plane, n_tp, *args):
    x, g, down, up, m1a, m2a, m1b, m2b, seeds_a, seeds_b, segments, bank = args
    rows = x.shape[0]
    ra, rb = m1a.shape[1], m1b.shape[1]
    width = up_to(ra, 128) + up_to(rb, 128)
    inverse = 1.0 / math.sqrt((x.shape[1] + g.shape[1]) * n_tp * down.shape[1])
    share = EXAMPLES * BANK // n_plane
    any_spec = pl.BlockSpec(memory_space=pl.ANY)
    vmem = pl.BlockSpec(memory_space=pltpu.VMEM)
    n_chip = n_plane // 2
    plane_sem = pltpu.SemaphoreType.DMA((n_chip, 2))
    tp_sem = pltpu.SemaphoreType.DMA((n_tp - 1,))
    like = lambda a: pltpu.VMEM(a.shape, a.dtype)
    return pl.pallas_call(
        functools.partial(kernel, n_ps, n_plane, n_tp, inverse),
        out_shape=jax.ShapeDtypeStruct((EXAMPLES, bank.shape[2]), F32),
        in_specs=[any_spec] * 8 + [vmem] * 3 + [any_spec],
        out_specs=vmem,
        scratch_shapes=[
            like(x), like(g), like(down), like(up), like(m1a), like(m2a), like(m1b), like(m2b), like(bank),
            pltpu.VMEM((n_plane, rows, width), BF16),
            pltpu.VMEM((n_plane, rows, width), BF16),
            pltpu.VMEM((rows, 256), F32),
            pltpu.VMEM((n_tp - 1, rows // n_tp, 256), F32),
            pltpu.VMEM((rows // n_tp, 256), BF16),
            pltpu.VMEM((n_plane, rows, 256), BF16),
            pltpu.VMEM((n_plane, rows, 128), F32),
            pltpu.VMEM((width, EXAMPLES * 128), F32),
            pltpu.VMEM((n_plane, share, 128), F32),
            pltpu.VMEM((n_plane, share, 128), F32),
            pltpu.VMEM((share, 128), F32),
            pltpu.VMEM((n_tp, share, 128), F32),
            pltpu.VMEM((n_plane, share, 128), F32),
            pltpu.VMEM((EXAMPLES * BANK, 128), F32),
            pltpu.SemaphoreType.DMA((9,)),
            plane_sem, plane_sem, tp_sem, tp_sem, tp_sem, tp_sem, plane_sem, plane_sem,
            plane_sem, plane_sem, tp_sem, tp_sem, plane_sem, plane_sem,
        ],
        compiler_params=pltpu.CompilerParams(
            collective_id=0, has_side_effects=True, vmem_limit_bytes=48 * 1024 * 1024
        ),
    )(x, g, down, up, m1a, m2a, m1b, m2b, seeds_a, seeds_b, segments.reshape(n_plane, rows), bank)


def solution(mesh):
    n_ps, n_tp = mesh.shape["ps"], mesh.shape["tp"]
    n_plane = mesh.shape["ex"] * n_ps
    return jax.shard_map(
        functools.partial(on_device, n_ps, n_plane, n_tp),
        mesh=mesh,
        in_specs=(
            P(("ex", "ps"), "tp"),
            P(("ex", "ps"), "tp"),
            P("tp", None),
            P("tp", None),
            P("tp", ("ex", "ps"), None),
            P("tp", ("ex", "ps"), None),
            P("tp", ("ex", "ps"), None),
            P("tp", ("ex", "ps"), None),
            P("tp", ("ex", "ps")),
            P("tp", ("ex", "ps")),
            P(),
            P(None, None, ("ex", "tp", "ps")),
        ),
        out_specs=P(None, ("ex", "tp", "ps")),
        check_vma=False,
    )
```

time: 123 us -> 65.9 us (0.54)
  blocking collectives: 78.5 us -> 0 us
  Pallas kernels: 0 us -> 55.5 us
  matrix products: 12 us -> 0 us
  starting transfers between devices: 9.49 us -> 0 us
  other arithmetic: 5.67 us -> 0 us
  local copies, waits for them, and re-layouts: 13.9 us -> 9.96 us
  waiting for transfers between devices: 2.63 us -> 0 us
    psum x2 -> x0, blocking collectives: 59.8 us -> none  [the longest x1 37.8 us: on_device(): summed = lax.psum(partial_value, ('ex', 'tp', 'ps'))]
    pallas_call x0 -> x1, Pallas kernels: none -> 55.5 us  [on_device(): pl.pallas_call(functools.partial(kernel, n_ps, n_plane, n_tp, inverse), o...]
    all_gather x2 -> x0, blocking collectives: 18.7 us -> none  [the longest x1 9.6 us: on_device(): lax.all_gather(input_inner_product, ('ex', 'ps'), axis=0, tiled=True)]
    dot_general x7 -> x0, matrix products: 12 us -> none  [the longest x2 4.26 us: contract_rows(): lax.dot_general(left, right, (((0,), (0,)), ((), ())), preferred_element_...]
    all_to_all x2 -> x0, starting transfers between devices: 9.49 us -> none  [the longest x1 5.17 us: on_device(): lax.all_to_all(tokens, ('ex', 'ps'), split_axis=1, concat_axis=0, tiled=T...]
    all_to_all x3 -> x0, local copies, waits for them, and re-layouts: 6.02 us -> none  [the longest x2 4.97 us: on_device(): lax.all_to_all(output_gradient, ('ex', 'ps'), split_axis=1, concat_axis=0...]
    unnamed x38 -> x22, local copies, waits for them, and re-layouts: 3.98 us -> 9.96 us
    mul x4 -> x0, other arithmetic: 4.65 us -> none  [the longest x1 2.94 us: spread_rows(): values[:, None, :] * picks[:, :, None]]
  transfers between devices with their start and end apart: 2 -> 0, of which waited for: 1 -> 0; matrix products, arithmetic and copies ran while one was open for 11% -> 0% of each run, Pallas kernels for 0% -> 0%
where the time goes in v1:
time: 65.9 us; the launch traced here: 65.6 us
  Pallas kernels  55.5 us (84%)
  local copies, waits for them, and re-layouts  9.96 us (15%)
    pallas_call x1, Pallas kernels, on_device(): pl.pallas_call(functools.partial(kernel, n_ps, n_plane, n_tp, inverse), o...  55.5 us
    unnamed x22, local copies, waits for them, and re-layouts  9.96 us

profile of v1, /device:TPU:0, one launch (start us, length us, event | category | flops | bytes accessed | tf_op | source)
XLA Modules:
  0.0 65.6 jit_solution(1133935368787773497)
XLA Ops:
  0.0 1.1 %copy.14.m1b_hbm = f32[1,924,128]{2,1,0:T(8,128)S(1)} copy(f32[1,924,128]{2,0,1:T(1,128)} %param.18) | data formatting | bytes 946176 | tf_op args[6]
  1.1 1.1 %copy.15.m2b_hbm = f32[1,924,128]{2,1,0:T(8,128)S(1)} copy(f32[1,924,128]{2,0,1:T(1,128)} %param.19) | data formatting | bytes 946176 | tf_op args[7]
  2.1 0.0 copy-start
  2.1 0.0 copy-start.2
  2.1 0.0 copy-start.4
  2.2 0.0 copy-start.6
  2.2 0.0 copy-start.7
  2.2 0.0 copy-start.8
  2.2 4.1 %copy.13.g_hbm = bf16[128,7392]{1,0:T(8,128)(2,1)} copy(bf16[128,7392]{0,1:T(8,128)(2,1)} %param.13) | data formatting | bytes 3784704 | tf_op args[1]
  6.2 0.0 copy-done
  6.2 0.0 copy-done.2
  6.2 0.0 copy-done.4
  6.3 0.0 copy-done.6
  6.3 0.0 copy-done.7
  6.3 0.0 copy-done.8
  6.3 0.0 copy-start.1
  6.3 1.2 %copy-done.1 = bf16[16,128,256]{2,1,0:T(8,128)(2,1)S(1)} copy-done((bf16[16,128,256]{2,1,0:T(8,128)(2,1)S(1)}, bf16[16,128,256]{2,1,0:T(8,128)(2,1)}, u32[]{:S(2)}) %copy-start.1) | copy-done | bytes 1048600
  7.5 0.0 copy-start.3
  7.5 1.0 %copy-done.3 = bf16[2048,128]{1,0:T(8,128)(2,1)S(1)} copy-done((bf16[2048,128]{1,0:T(8,128)(2,1)S(1)}, bf16[2048,128]{1,0:T(8,128)(2,1)}, u32[]{:S(2)}) %copy-start.3) | copy-done | bytes 524312
  8.6 0.0 copy-start.5
  8.6 0.9 %copy-done.5 = f32[1,256,128]{2,1,0:T(8,128)S(1)} copy-done((f32[1,256,128]{2,1,0:T(8,128)S(1)}, f32[1,256,128]{2,1,0:T(8,128)}, u32[]{:S(2)}) %copy-start.5) | copy-done | bytes 131096
  9.5 55.5 %shard_map.118 = f32[4,256]{1,0:T(4,128)S(1)} custom-call(bf16[128,2048]{1,0:T(8,128)(2,1)S(1)} %copy-done.2, bf16[128,7392]{1,0:T(8,128)(2,1)} %copy.13.g_hbm, bf16[2048,128]{1,0:T(8,128)(2,1)S(1)} %copy-done.3, bf16[7392,128]{1,0:T(8,128)(2,1)S(1)} %copy-done, f32[1,256,128]{2,1,0:T(8,128)S(1)} %copy-done.4, f32[1,256,128]{2,1,0:T(8,128)S(1)} %copy-done.5, ...), custom_call_target="tpu_custom_call" | custom-call | tf_op jit(solution)/shard_map/pallas_call | solution.py:249
  65.0 0.6 copy.17
Async XLA Ops:
  2.1 4.1 %copy-start = (bf16[7392,128]{1,0:T(8,128)(2,1)S(1)}, bf16[7392,128]{1,0:T(8,128)(2,1)}, u32[]{:S(2)}) copy-start(bf16[7392,128]{1,0:T(8,128)(2,1)} %up_hbm.1) | copy-start | bytes 5677060
  2.1 4.1 %copy-start.2 = (bf16[128,2048]{1,0:T(8,128)(2,1)S(1)}, bf16[128,2048]{1,0:T(8,128)(2,1)}, u32[]{:S(2)}) copy-start(bf16[128,2048]{1,0:T(8,128)(2,1)} %x_hbm.1) | copy-start | bytes 1572868
  2.1 4.1 %copy-start.4 = (f32[1,256,128]{2,1,0:T(8,128)S(1)}, f32[1,256,128]{2,1,0:T(8,128)}, u32[]{:S(2)}) copy-start(f32[1,256,128]{2,1,0:T(8,128)} %m1a_hbm.1) | copy-start | bytes 393220
  2.2 4.1 %copy-start.6 = (s32[1,924]{1,0:T(1,128)S(1)}, s32[1,924]{1,0:T(1,128)}, u32[]{:S(2)}) copy-start(s32[1,924]{1,0:T(1,128)} %seeds_b.1) | copy-start | bytes 11092
  2.2 4.1 %copy-start.7 = (s32[1024]{0:T(1024)S(1)}, s32[1024]{0:T(1024)}, u32[]{:S(2)}) copy-start(s32[1024]{0:T(1024)} %param.22) | copy-start | bytes 12292
  2.2 4.1 %copy-start.8 = (s32[1,256]{1,0:T(1,128)S(1)}, s32[1,256]{1,0:T(1,128)}, u32[]{:S(2)}) copy-start(s32[1,256]{1,0:T(1,128)} %seeds_a.1) | copy-start | bytes 3076
  6.3 1.2 %copy-start.1 = (bf16[16,128,256]{2,1,0:T(8,128)(2,1)S(1)}, bf16[16,128,256]{2,1,0:T(8,128)(2,1)}, u32[]{:S(2)}) copy-start(bf16[16,128,256]{2,1,0:T(8,128)(2,1)} %bank_hbm.1) | copy-start | bytes 3145732
  7.5 1.0 %copy-start.3 = (bf16[2048,128]{1,0:T(8,128)(2,1)S(1)}, bf16[2048,128]{1,0:T(8,128)(2,1)}, u32[]{:S(2)}) copy-start(bf16[2048,128]{1,0:T(8,128)(2,1)} %down_hbm.1) | copy-start | bytes 1572868
  8.6 0.9 %copy-start.5 = (f32[1,256,128]{2,1,0:T(8,128)S(1)}, f32[1,256,128]{2,1,0:T(8,128)}, u32[]{:S(2)}) copy-start(f32[1,256,128]{2,1,0:T(8,128)} %m2a_hbm.1) | copy-start | bytes 393220

commit v2 on v1

v2 whole, which is shorter than its diff:
```python
import functools
import math

import jax
import jax.numpy as jnp
from jax import lax
from jax.experimental import pallas as pl
from jax.experimental.pallas import tpu as pltpu
from jax.sharding import PartitionSpec as P

EXAMPLES = 4
BANK = 16
MESH = pl.DeviceIdType.MESH
F32 = jnp.float32
BF16 = jnp.bfloat16


def flip(index, mask):
    out, bit = index, 1
    while bit <= mask:
        if mask & bit:
            out = out + bit - 2 * bit * ((index // bit) % 2)
        bit *= 2
    return out


def up_to(value, step):
    return -(-value // step) * step


def contract_rows(left, right):
    return lax.dot_general(left, right, (((0,), (0,)), ((), ())), preferred_element_type=F32)


def split(value, parts):
    out = []
    for _ in range(parts):
        piece = value.astype(BF16)
        out.append(piece)
        value = value - piece.astype(F32)
    return out


def pieces_of(rb):
    blocks = -(-rb // 128)
    ends = [min(rb, 128 * -(-blocks * i // 3)) for i in range(4)]
    return [(lo, hi) for lo, hi in zip(ends[:-1], ends[1:]) if hi > lo]


def kernel(
    n_ps, n_plane, n_tp, inverse,
    x_hbm, g_hbm, down_hbm, up_hbm, m1a_hbm, m2a_hbm, m1b_hbm, m2b_hbm, seeds_a, seeds_b, segments, bank_hbm,
    out_ref,
    x, g, down, up, m1a, m2a, m1b, m2b, bank,
    stage_a, recv_a, stage_b, recv_b, part, part_in, rank_sum, ranks, picked_h, picked_u,
    sums, sums_in, mine, mine_in, total_in, total,
    load_sem, a_send, a_recv, b_send, b_recv, rs_send, rs_recv, ag_send, ag_recv, pl_send, pl_recv,
    s1_send, s1_recv, s2_send, s2_recv, s3_send, s3_recv,
):
    ex, tp, ps = lax.axis_index("ex"), lax.axis_index("tp"), lax.axis_index("ps")
    q = ex * n_ps + ps
    chip, core = q // 2, q % 2
    n_chip = n_plane // 2
    rows = x.shape[0]
    ra, rb = m1a.shape[1], m1b.shape[0]

    pairs = [(x_hbm, x), (g_hbm, g), (down_hbm, down), (up_hbm, up), (m1a_hbm, m1a), (m2a_hbm, m2a),
             (m1b_hbm.at[:, 0, :], m1b), (m2b_hbm.at[:, 0, :], m2b), (bank_hbm, bank)]
    loads = [pltpu.make_async_copy(a, b, load_sem.at[i]) for i, (a, b) in enumerate(pairs)]
    for i in (1, 0, 2, 3, 4, 5, 6, 7, 8):
        loads[i].start()

    def plane_id(peer):
        return {"ex": peer // n_ps, "ps": peer % n_ps}

    def tp_id(d):
        return {"tp": (tp + d) % n_tp}

    peers = [(mask, other) for mask in range(n_chip) for other in range(2) if mask or other]

    def peer_of(mask, other):
        return 2 * flip(chip, mask) + (core + other) % 2

    barrier = pltpu.get_barrier_semaphore()
    for mask, other in peers:
        pl.semaphore_signal(barrier, inc=1, device_id=plane_id(peer_of(mask, other)), device_id_type=MESH)
    for d in range(1, n_tp):
        pl.semaphore_signal(barrier, inc=1, device_id=tp_id(d), device_id_type=MESH)

    def plane_copies(src, dst, send, recv_sem, chosen):
        return [
            pltpu.make_async_remote_copy(
                src_ref=src(peer_of(mask, other)), dst_ref=dst, send_sem=send.at[mask, other],
                recv_sem=recv_sem.at[mask, other], device_id=plane_id(peer_of(mask, other)), device_id_type=MESH,
            )
            for mask, other in chosen
        ]

    loads[1].wait()
    spans = pieces_of(rb)
    b_copies = []
    for i, (lo, hi) in enumerate(spans):
        for j in range(n_plane):
            stage_b[j, lo:hi, :] = g[j * rb + lo:j * rb + hi, :]
        window = pl.ds(lo, up_to(hi, 16) - lo)
        b_copies.append(plane_copies(
            lambda peer: stage_b.at[peer, window], recv_b.at[q, window], b_send.at[i], b_recv.at[i], peers
        ))
        if i == 0:
            pl.semaphore_wait(barrier, n_plane - 1 + n_tp - 1)
        if i < len(spans) - 1:
            for copy in b_copies[i]:
                copy.start()

    loads[0].wait()
    loads[2].wait()
    loads[3].wait()
    part[:, 0:128] = jnp.dot(x[...], down[...], preferred_element_type=F32)
    part[:, 128:256] = contract_rows(g[...], up[...])
    slab = rows // n_tp

    def slab_at(t):
        return pl.ds(pl.multiple_of(t * slab, slab), slab)

    rs = [
        pltpu.make_async_remote_copy(
            src_ref=part.at[slab_at((tp + d) % n_tp)], dst_ref=part_in.at[d - 1], send_sem=rs_send.at[d - 1],
            recv_sem=rs_recv.at[d - 1], device_id=tp_id(d), device_id_type=MESH,
        )
        for d in range(1, n_tp)
    ]
    for copy in rs:
        copy.start()

    for j in range(n_plane):
        stage_a[j, :, 0:ra] = x[:, j * ra:(j + 1) * ra]
    a_copies = plane_copies(lambda peer: stage_a.at[peer], recv_a.at[q], a_send, a_recv, peers)
    recv_a[q] = stage_a[q]
    recv_b[q] = stage_b[q]
    seg = segments[...]
    inv_len = [1.0 / jnp.sum((seg == e).astype(F32), axis=(0, 1), keepdims=True) for e in range(EXAMPLES)]
    seg_t = jnp.transpose(seg.astype(F32))

    for copy in rs:
        copy.wait()
    summed = part[slab_at(tp), :]
    for d in range(1, n_tp):
        summed = summed + part_in[d - 1]
    rank_sum[...] = summed.astype(BF16)
    ranks[q, slab_at(tp), :] = rank_sum[...]
    ag = [
        pltpu.make_async_remote_copy(
            src_ref=rank_sum, dst_ref=ranks.at[q, slab_at(tp)], send_sem=ag_send.at[d - 1],
            recv_sem=ag_recv.at[d - 1], device_id=tp_id(d), device_id_type=MESH,
        )
        for d in range(1, n_tp)
    ]
    for copy in ag:
        copy.start()
    for copy in ag:
        copy.wait()

    far = plane_copies(lambda peer: ranks.at[q], ranks.at[q], pl_send, pl_recv, [(m, 0) for m in range(1, n_chip)])
    near = []
    for mask in range(n_chip):
        slot = ranks.at[2 * flip(chip, mask) + core]
        near += plane_copies(lambda peer: slot, slot, pl_send.at[pl.ds(mask, 1)], pl_recv.at[pl.ds(mask, 1)], [(0, 1)])
    for copy in far + near[:1] + a_copies + b_copies[-1]:
        copy.start()
    for arrived, onward in zip(far, near[1:]):
        arrived.wait()
        onward.start()
    for copy in near:
        copy.wait()

    for j in range(n_plane):
        both = ranks[j].astype(F32)
        label = jnp.broadcast_to(seg_t[:, j:j + 1], (rows, 256))
        for e in range(EXAMPLES):
            chosen = jnp.where(label == e, both, 0.0).astype(BF16)
            picked_h[j * rows:(j + 1) * rows, e * 128:(e + 1) * 128] = chosen[:, 0:128]
            picked_u[j * rows:(j + 1) * rows, e * 128:(e + 1) * 128] = chosen[:, 128:256]

    for load in loads[4:]:
        load.wait()
    bins = lax.broadcasted_iota(jnp.int32, (BANK, 128), 0)
    block_sums = [jnp.zeros((BANK, 128), F32) for _ in range(EXAMPLES)]

    def add_features(grads, m1, m2, seeds, size):
        first = 0.9 * m1
        second = 0.999 * m2
        select = (seeds == bins[:, :size]).astype(BF16)
        for e in range(EXAMPLES):
            grad = grads[:, e * 128:(e + 1) * 128] * inv_len[e]
            moved = first + 0.1 * grad
            scaled = second + 0.001 * grad * grad
            bottom = scaled * lax.rsqrt(scaled) + 1e-08
            guess = pl.reciprocal(bottom, approx=True)
            feature = moved * (guess * (2.0 - bottom * guess))
            for piece in split(feature, 2):
                block_sums[e] = block_sums[e] + jnp.dot(select, piece, preferred_element_type=F32)

    def up_rows(index):
        for copy in b_copies[index]:
            copy.wait()
        low, high = spans[index]
        for lo in range(low, high, 128):
            hi = min(lo + 128, high)
            block = jnp.concatenate([recv_b[j, lo:hi, :] for j in range(n_plane)], axis=1)
            grads = jnp.dot(block, picked_h[...], preferred_element_type=F32)
            add_features(grads, m1b[lo:hi, :], m2b[lo:hi, :], seeds_b[:, lo:hi], hi - lo)

    for index in range(len(spans) - 1):
        up_rows(index)
    for copy in a_copies:
        copy.wait()
    for lo in range(0, ra, 128):
        hi = min(lo + 128, ra)
        block = recv_a[:, :, lo:hi].reshape(n_plane * rows, hi - lo)
        grads = contract_rows(block, picked_u[...])
        add_features(grads, m1a[0, lo:hi, :], m2a[0, lo:hi, :], seeds_a[:, lo:hi], hi - lo)
    up_rows(len(spans) - 1)
    summed = block_sums

    share = sums.shape[1]
    every = jnp.concatenate(summed, axis=0)
    for j in range(n_plane):
        sums[j] = every[j * share:(j + 1) * share, :]
    scatter = plane_copies(lambda peer: sums.at[peer], sums_in.at[q], s1_send, s1_recv, peers)
    for copy in scatter:
        copy.start()
    sums_in[q] = sums[q]
    for copy in scatter:
        copy.wait()
    mine[...] = jnp.sum(sums_in[...], axis=0)
    cross = [
        pltpu.make_async_remote_copy(
            src_ref=mine, dst_ref=mine_in.at[tp], send_sem=s2_send.at[d - 1], recv_sem=s2_recv.at[d - 1],
            device_id=tp_id(d), device_id_type=MESH,
        )
        for d in range(1, n_tp)
    ]
    for copy in cross:
        copy.start()
    mine_in[tp] = mine[...]
    for copy in cross:
        copy.wait()
    total_in[q] = jnp.sum(mine_in[...], axis=0)
    spread = plane_copies(lambda peer: total_in.at[q], total_in.at[q], s3_send, s3_recv, peers)
    for copy in spread:
        copy.start()
    for copy in spread:
        copy.wait()
    for j in range(n_plane):
        total[j * share:(j + 1) * share, :] = total_in[j]

    flat = jnp.concatenate([total[pl.ds(j, EXAMPLES, stride=BANK), :] for j in range(BANK)], axis=1)
    bank_rows = bank[...].reshape(BANK * 128, bank.shape[2])
    high = flat.astype(BF16).astype(F32)
    both = jnp.concatenate([high, flat - high], axis=0).astype(BF16)
    result = jnp.dot(both, bank_rows, preferred_element_type=F32)
    out_ref[...] = (result[:EXAMPLES] + result[EXAMPLES:]) * inverse


def on_device(n_ps, n_plane, n_tp, *args):
    x, g, down, up, m1a, m2a, m1b, m2b, seeds_a, seeds_b, segments, bank = args
    rows = x.shape[0]
    ra, rb = m1a.shape[1], m1b.shape[1]
    pa, pb = up_to(ra, 128), up_to(rb, 16)
    g = g.T
    m1b, m2b = jnp.swapaxes(m1b, 0, 1), jnp.swapaxes(m2b, 0, 1)
    inverse = 1.0 / math.sqrt((x.shape[1] + g.shape[0]) * n_tp * down.shape[1])
    share = EXAMPLES * BANK // n_plane
    any_spec = pl.BlockSpec(memory_space=pltpu.HBM)
    vmem = pl.BlockSpec(memory_space=pltpu.VMEM)
    n_chip = n_plane // 2
    plane_sem = pltpu.SemaphoreType.DMA((n_chip, 2))
    piece_sem = pltpu.SemaphoreType.DMA((len(pieces_of(rb)), n_chip, 2))
    tp_sem = pltpu.SemaphoreType.DMA((n_tp - 1,))
    like = lambda a: pltpu.VMEM(a.shape, a.dtype)
    return pl.pallas_call(
        functools.partial(kernel, n_ps, n_plane, n_tp, inverse),
        out_shape=jax.ShapeDtypeStruct((EXAMPLES, bank.shape[2]), F32),
        in_specs=[any_spec] * 8 + [vmem] * 3 + [any_spec],
        out_specs=vmem,
        scratch_shapes=[
            like(x), like(g), like(down), like(up), like(m1a), like(m2a), pltpu.VMEM((rb, 128), F32), pltpu.VMEM((rb, 128), F32), like(bank),
            pltpu.VMEM((n_plane, rows, pa), BF16),
            pltpu.VMEM((n_plane, rows, pa), BF16),
            pltpu.VMEM((n_plane, pb, 128), BF16),
            pltpu.VMEM((n_plane, pb, 128), BF16),
            pltpu.VMEM((rows, 256), F32),
            pltpu.VMEM((n_tp - 1, rows // n_tp, 256), F32),
            pltpu.VMEM((rows // n_tp, 256), BF16),
            pltpu.VMEM((n_plane, rows, 256), BF16),
            pltpu.VMEM((n_plane * rows, EXAMPLES * 128), BF16),
            pltpu.VMEM((n_plane * rows, EXAMPLES * 128), BF16),
            pltpu.VMEM((n_plane, share, 128), F32),
            pltpu.VMEM((n_plane, share, 128), F32),
            pltpu.VMEM((share, 128), F32),
            pltpu.VMEM((n_tp, share, 128), F32),
            pltpu.VMEM((n_plane, share, 128), F32),
            pltpu.VMEM((EXAMPLES * BANK, 128), F32),
            pltpu.SemaphoreType.DMA((9,)),
            plane_sem, plane_sem, piece_sem, piece_sem, tp_sem, tp_sem, tp_sem, tp_sem, plane_sem, plane_sem,
            plane_sem, plane_sem, tp_sem, tp_sem, plane_sem, plane_sem,
        ],
        compiler_params=pltpu.CompilerParams(
            collective_id=0, has_side_effects=True, vmem_limit_bytes=63 * 1024 * 1024
        ),
    )(x, g, down, up, m1a, m2a, m1b, m2b, seeds_a, seeds_b, segments.reshape(n_plane, rows), bank)


def solution(mesh):
    n_ps, n_tp = mesh.shape["ps"], mesh.shape["tp"]
    n_plane = mesh.shape["ex"] * n_ps
    return jax.shard_map(
        functools.partial(on_device, n_ps, n_plane, n_tp),
        mesh=mesh,
        in_specs=(
            P(("ex", "ps"), "tp"),
            P(("ex", "ps"), "tp"),
            P("tp", None),
            P("tp", None),
            P("tp", ("ex", "ps"), None),
            P("tp", ("ex", "ps"), None),
            P("tp", ("ex", "ps"), None),
            P("tp", ("ex", "ps"), None),
            P("tp", ("ex", "ps")),
            P("tp", ("ex", "ps")),
            P(),
            P(None, None, ("ex", "tp", "ps")),
        ),
        out_specs=P(None, ("ex", "tp", "ps")),
        check_vma=False,
    )
```

time: 65.9 us -> 51.6 us (0.78)
  local copies, waits for them, and re-layouts: 9.96 us -> 1.28 us
  Pallas kernels: 55.5 us -> 50.1 us
    unnamed x22 -> x1, local copies, waits for them, and re-layouts: 9.96 us -> 1.28 us
    pallas_call x1, Pallas kernels: 55.5 us -> 50.1 us  [on_device(): pl.pallas_call(functools.partial(kernel, n_ps, n_plane, n_tp, inverse), o...]
where the time goes in v2:
time: 51.6 us; the launch traced here: 51.4 us
  Pallas kernels  50.1 us (97%)
  local copies, waits for them, and re-layouts  1.28 us (2%)
    pallas_call x1, Pallas kernels, on_device(): pl.pallas_call(functools.partial(kernel, n_ps, n_plane, n_tp, inverse), o...  50.1 us
    unnamed x1, local copies, waits for them, and re-layouts  1.28 us

profile of v2, /device:TPU:0, one launch (start us, length us, event | category | flops | bytes accessed | tf_op | source)
XLA Modules:
  0.0 51.4 jit_solution(17269766000897231985)
XLA Ops:
  0.0 50.1 %shard_map.118 = f32[4,256]{1,0:T(4,128)} custom-call(bf16[128,2048]{1,0:T(8,128)(2,1)} %x_hbm.1, bf16[7392,128]{1,0:T(8,128)(2,1)} %bitcast.4, bf16[2048,128]{1,0:T(8,128)(2,1)} %down_hbm.1, bf16[7392,128]{1,0:T(8,128)(2,1)} %up_hbm.1, f32[1,256,128]{2,1,0:T(8,128)} %m1a_hbm.1, f32[1,256,128]{2,1,0:T(8,128)} %m2a_hbm.1, f32[924,1,128]{2,1,0:T(1,128)} %bitcast.5, ...), custom_call_target="tpu_custom_call" | custom-call | tf_op jit(solution)/shard_map/pallas_call | solution.py:281
  50.1 1.3 %copy.14 = f32[4,256]{1,0:T(4,128)} copy(f32[4,256]{1,0:T(4,128)} %shard_map.118) | data formatting | bytes 8192

commit v3 on v2

--- a/solution.py
+++ b/solution.py
@@ -49,9 +49,10 @@
 
 def kernel(
     n_ps, n_plane, n_tp, inverse,
-    x_hbm, g_hbm, down_hbm, up_hbm, m1a_hbm, m2a_hbm, m1b_hbm, m2b_hbm, seeds_a, seeds_b, segments, bank_hbm,
+    x_hbm, g_hbm, down_hbm, up_hbm, m1a_hbm, m2a_hbm, m1b_hbm, m2b_hbm, seeds_a_hbm, seeds_b_hbm, segments_hbm,
+    bank_hbm,
     out_ref,
-    x, g, down, up, m1a, m2a, m1b, m2b, bank,
+    x, g, down, up, m1a, m2a, m1b, m2b, bank, seeds_a, seeds_b, segments,
     stage_a, recv_a, stage_b, recv_b, part, part_in, rank_sum, ranks, picked_h, picked_u,
     sums, sums_in, mine, mine_in, total_in, total,
     load_sem, a_send, a_recv, b_send, b_recv, rs_send, rs_recv, ag_send, ag_recv, pl_send, pl_recv,
@@ -65,10 +66,9 @@
     ra, rb = m1a.shape[1], m1b.shape[0]
 
     pairs = [(x_hbm, x), (g_hbm, g), (down_hbm, down), (up_hbm, up), (m1a_hbm, m1a), (m2a_hbm, m2a),
-             (m1b_hbm.at[:, 0, :], m1b), (m2b_hbm.at[:, 0, :], m2b), (bank_hbm, bank)]
+             (m1b_hbm.at[:, 0, :], m1b), (m2b_hbm.at[:, 0, :], m2b), (bank_hbm, bank),
+             (seeds_a_hbm, seeds_a), (seeds_b_hbm, seeds_b), (segments_hbm, segments)]
     loads = [pltpu.make_async_copy(a, b, load_sem.at[i]) for i, (a, b) in enumerate(pairs)]
-    for i in (1, 0, 2, 3, 4, 5, 6, 7, 8):
-        loads[i].start()
 
     def plane_id(peer):
         return {"ex": peer // n_ps, "ps": peer % n_ps}
@@ -86,6 +86,8 @@
         pl.semaphore_signal(barrier, inc=1, device_id=plane_id(peer_of(mask, other)), device_id_type=MESH)
     for d in range(1, n_tp):
         pl.semaphore_signal(barrier, inc=1, device_id=tp_id(d), device_id_type=MESH)
+    for i in (1, 3, 0, 2, 11, 4, 5, 6, 7, 8, 9, 10):
+        loads[i].start()
 
     def plane_copies(src, dst, send, recv_sem, chosen):
         return [
@@ -96,7 +98,46 @@
             for mask, other in chosen
         ]
 
+    direct = ra % 128 == 0
+    if direct:
+        def columns(peer):
+            return x_hbm.at[:, pl.ds(pl.multiple_of(peer * ra, ra), ra)]
+        own = pltpu.make_async_copy(columns(q), recv_a.at[q], load_sem.at[len(loads)])
+        own.start()
+    else:
+        loads[0].wait()
+        for j in range(n_plane):
+            stage_a[j, :, 0:ra] = x[:, j * ra:(j + 1) * ra]
+        recv_a[q] = stage_a[q]
+    a_copies = plane_copies(
+        columns if direct else (lambda peer: stage_a.at[peer]), recv_a.at[q], a_send, a_recv, peers
+    )
+    pl.semaphore_wait(barrier, n_plane - 1 + n_tp - 1)
+    for copy in a_copies:
+        copy.start()
+
     loads[1].wait()
+    loads[3].wait()
+    part[:, 128:256] = contract_rows(g[...], up[...])
+    if direct:
+        loads[0].wait()
+    loads[2].wait()
+    part[:, 0:128] = jnp.dot(x[...], down[...], preferred_element_type=F32)
+    slab = rows // n_tp
+
+    def slab_at(t):
+        return pl.ds(pl.multiple_of(t * slab, slab), slab)
+
+    rs = [
+        pltpu.make_async_remote_copy(
+            src_ref=part.at[slab_at((tp + d) % n_tp)], dst_ref=part_in.at[d - 1], send_sem=rs_send.at[d - 1],
+            recv_sem=rs_recv.at[d - 1], device_id=tp_id(d), device_id_type=MESH,
+        )
+        for d in range(1, n_tp)
+    ]
+    for copy in rs:
+        copy.start()
+
     spans = pieces_of(rb)
     b_copies = []
     for i, (lo, hi) in enumerate(spans):
@@ -107,38 +148,14 @@
             lambda peer: stage_b.at[peer, window], recv_b.at[q, window], b_send.at[i], b_recv.at[i], peers
         ))
         if i == 0:
-            pl.semaphore_wait(barrier, n_plane - 1 + n_tp - 1)
-        if i < len(spans) - 1:
-            for copy in b_copies[i]:
+            for copy in b_copies[0]:
                 copy.start()
-
-    loads[0].wait()
-    loads[2].wait()
-    loads[3].wait()
-    part[:, 0:128] = jnp.dot(x[...], down[...], preferred_element_type=F32)
-    part[:, 128:256] = contract_rows(g[...], up[...])
-    slab = rows // n_tp
-
-    def slab_at(t):
-        return pl.ds(pl.multiple_of(t * slab, slab), slab)
-
-    rs = [
-        pltpu.make_async_remote_copy(
-            src_ref=part.at[slab_at((tp + d) % n_tp)], dst_ref=part_in.at[d - 1], send_sem=rs_send.at[d - 1],
-            recv_sem=rs_recv.at[d - 1], device_id=tp_id(d), device_id_type=MESH,
-        )
-        for d in range(1, n_tp)
-    ]
-    for copy in rs:
-        copy.start()
-
-    for j in range(n_plane):
-        stage_a[j, :, 0:ra] = x[:, j * ra:(j + 1) * ra]
-    a_copies = plane_copies(lambda peer: stage_a.at[peer], recv_a.at[q], a_send, a_recv, peers)
-    recv_a[q] = stage_a[q]
     recv_b[q] = stage_b[q]
+    loads[11].wait()
     seg = segments[...]
     inv_len = [1.0 / jnp.sum((seg == e).astype(F32), axis=(0, 1), keepdims=True) for e in range(EXAMPLES)]
+    tenth = [0.1 * value for value in inv_len]
+    small = [0.001 * value * value for value in inv_len]
     seg_t = jnp.transpose(seg.astype(F32))
 
     for copy in rs:
@@ -165,7 +182,7 @@
     for mask in range(n_chip):
         slot = ranks.at[2 * flip(chip, mask) + core]
         near += plane_copies(lambda peer: slot, slot, pl_send.at[pl.ds(mask, 1)], pl_recv.at[pl.ds(mask, 1)], [(0, 1)])
-    for copy in far + near[:1] + a_copies + b_copies[-1]:
+    for copy in far + near[:1] + [copy for piece in b_copies[1:] for copy in piece]:
         copy.start()
     for arrived, onward in zip(far, near[1:]):
         arrived.wait()
@@ -181,7 +198,7 @@
             picked_h[j * rows:(j + 1) * rows, e * 128:(e + 1) * 128] = chosen[:, 0:128]
             picked_u[j * rows:(j + 1) * rows, e * 128:(e + 1) * 128] = chosen[:, 128:256]
 
-    for load in loads[4:]:
+    for load in loads[4:11]:
         load.wait()
     bins = lax.broadcasted_iota(jnp.int32, (BANK, 128), 0)
     block_sums = [jnp.zeros((BANK, 128), F32) for _ in range(EXAMPLES)]
@@ -191,9 +208,9 @@
         second = 0.999 * m2
         select = (seeds == bins[:, :size]).astype(BF16)
         for e in range(EXAMPLES):
-            grad = grads[:, e * 128:(e + 1) * 128] * inv_len[e]
-            moved = first + 0.1 * grad
-            scaled = second + 0.001 * grad * grad
+            grad = grads[:, e * 128:(e + 1) * 128]
+            moved = first + tenth[e] * grad
+            scaled = second + small[e] * (grad * grad)
             bottom = scaled * lax.rsqrt(scaled) + 1e-08
             guess = pl.reciprocal(bottom, approx=True)
             feature = moved * (guess * (2.0 - bottom * guess))
@@ -210,16 +227,17 @@
             grads = jnp.dot(block, picked_h[...], preferred_element_type=F32)
             add_features(grads, m1b[lo:hi, :], m2b[lo:hi, :], seeds_b[:, lo:hi], hi - lo)
 
-    for index in range(len(spans) - 1):
-        up_rows(index)
     for copy in a_copies:
         copy.wait()
+    if direct:
+        own.wait()
     for lo in range(0, ra, 128):
         hi = min(lo + 128, ra)
         block = recv_a[:, :, lo:hi].reshape(n_plane * rows, hi - lo)
         grads = contract_rows(block, picked_u[...])
         add_features(grads, m1a[0, lo:hi, :], m2a[0, lo:hi, :], seeds_a[:, lo:hi], hi - lo)
-    up_rows(len(spans) - 1)
+    for index in range(len(spans)):
+        up_rows(index)
     summed = block_sums
 
     share = sums.shape[1]
@@ -281,10 +299,11 @@
     return pl.pallas_call(
         functools.partial(kernel, n_ps, n_plane, n_tp, inverse),
         out_shape=jax.ShapeDtypeStruct((EXAMPLES, bank.shape[2]), F32),
-        in_specs=[any_spec] * 8 + [vmem] * 3 + [any_spec],
+        in_specs=[any_spec] * 12,
         out_specs=vmem,
         scratch_shapes=[
             like(x), like(g), like(down), like(up), like(m1a), like(m2a), pltpu.VMEM((rb, 128), F32), pltpu.VMEM((rb, 128), F32), like(bank),
+            like(seeds_a), like(seeds_b), pltpu.VMEM((n_plane, rows), jnp.int32),
             pltpu.VMEM((n_plane, rows, pa), BF16),
             pltpu.VMEM((n_plane, rows, pa), BF16),
             pltpu.VMEM((n_plane, pb, 128), BF16),
@@ -301,7 +320,7 @@
             pltpu.VMEM((n_tp, share, 128), F32),
             pltpu.VMEM((n_plane, share, 128), F32),
             pltpu.VMEM((EXAMPLES * BANK, 128), F32),
-            pltpu.SemaphoreType.DMA((9,)),
+            pltpu.SemaphoreType.DMA((13,)),
             plane_sem, plane_sem, piece_sem, piece_sem, tp_sem, tp_sem, tp_sem, tp_sem, plane_sem, plane_sem,
             plane_sem, plane_sem, tp_sem, tp_sem, plane_sem, plane_sem,
         ],

time: 51.6 us -> 50.3 us (0.975)
  Pallas kernels: 50.1 us -> 48.8 us
    pallas_call x1, Pallas kernels: 50.1 us -> 48.8 us  [on_device(): pl.pallas_call(functools.partial(kernel, n_ps, n_plane, n_tp, inverse), o...]
where the time goes in v3:
time: 50.3 us; the launch traced here: 50.1 us
  Pallas kernels  48.8 us (97%)
  local copies, waits for them, and re-layouts  1.28 us (3%)
    pallas_call x1, Pallas kernels, on_device(): pl.pallas_call(functools.partial(kernel, n_ps, n_plane, n_tp, inverse), o...  48.8 us
    unnamed x1, local copies, waits for them, and re-layouts  1.28 us

profile of v3, /device:TPU:0, one launch (start us, length us, event | category | flops | bytes accessed | tf_op | source)
XLA Modules:
  0.0 50.1 jit_solution(16580143436835375252)
XLA Ops:
  0.0 48.8 %shard_map.118 = f32[4,256]{1,0:T(4,128)} custom-call(bf16[128,2048]{1,0:T(8,128)(2,1)} %x_hbm.1, bf16[7392,128]{1,0:T(8,128)(2,1)} %bitcast.4, bf16[2048,128]{1,0:T(8,128)(2,1)} %down_hbm.1, bf16[7392,128]{1,0:T(8,128)(2,1)} %up_hbm.1, f32[1,256,128]{2,1,0:T(8,128)} %m1a_hbm.1, f32[1,256,128]{2,1,0:T(8,128)} %m2a_hbm.1, f32[924,1,128]{2,1,0:T(1,128)} %bitcast.5, ...), custom_call_target="tpu_custom_call" | custom-call | tf_op jit(solution)/shard_map/pallas_call | solution.py:299
  48.8 1.3 %copy.14 = f32[4,256]{1,0:T(4,128)} copy(f32[4,256]{1,0:T(4,128)} %shard_map.118) | data formatting | bytes 8192

commit v4 on v3

--- a/solution.py
+++ b/solution.py
@@ -201,44 +201,49 @@
     for load in loads[4:11]:
         load.wait()
     bins = lax.broadcasted_iota(jnp.int32, (BANK, 128), 0)
-    block_sums = [jnp.zeros((BANK, 128), F32) for _ in range(EXAMPLES)]
-
-    def add_features(grads, m1, m2, seeds, size):
+    block_sums = jnp.zeros((BANK, EXAMPLES * 128), F32)
+
+    def add_features(block_sums, grads, m1, m2, seeds, size):
         first = 0.9 * m1
         second = 0.999 * m2
         select = (seeds == bins[:, :size]).astype(BF16)
+        features = []
         for e in range(EXAMPLES):
             grad = grads[:, e * 128:(e + 1) * 128]
             moved = first + tenth[e] * grad
             scaled = second + small[e] * (grad * grad)
             bottom = scaled * lax.rsqrt(scaled) + 1e-08
             guess = pl.reciprocal(bottom, approx=True)
-            feature = moved * (guess * (2.0 - bottom * guess))
-            for piece in split(feature, 2):
-                block_sums[e] = block_sums[e] + jnp.dot(select, piece, preferred_element_type=F32)
-
-    def up_rows(index):
-        for copy in b_copies[index]:
+            features.append(split(moved * (guess * (2.0 - bottom * guess)), 2))
+        high, low = (jnp.concatenate([feature[i] for feature in features], axis=1) for i in range(2))
+        if size == 128:
+            twice = jnp.concatenate([select, select], axis=1)
+            return block_sums + jnp.dot(twice, jnp.concatenate([high, low], axis=0), preferred_element_type=F32)
+        block_sums = block_sums + jnp.dot(select, high, preferred_element_type=F32)
+        return block_sums + jnp.dot(select, low, preferred_element_type=F32)
+
+    for copy in a_copies:
+        copy.wait()
+    if direct:
+        own.wait()
+    block = recv_a[:, :, 0:ra].reshape(n_plane * rows, ra)
+    grads = contract_rows(block, picked_u[...])
+    for lo in range(0, ra, 128):
+        hi = min(lo + 128, ra)
+        block_sums = add_features(
+            block_sums, grads[lo:hi], m1a[0, lo:hi, :], m2a[0, lo:hi, :], seeds_a[:, lo:hi], hi - lo
+        )
+    for (low, high), copies in zip(spans, b_copies):
+        for copy in copies:
             copy.wait()
-        low, high = spans[index]
+        block = jnp.concatenate([recv_b[j, low:high, :] for j in range(n_plane)], axis=1)
+        grads = jnp.dot(block, picked_h[...], preferred_element_type=F32)
         for lo in range(low, high, 128):
             hi = min(lo + 128, high)
-            block = jnp.concatenate([recv_b[j, lo:hi, :] for j in range(n_plane)], axis=1)
-            grads = jnp.dot(block, picked_h[...], preferred_element_type=F32)
-            add_features(grads, m1b[lo:hi, :], m2b[lo:hi, :], seeds_b[:, lo:hi], hi - lo)
-
-    for copy in a_copies:
-        copy.wait()
-    if direct:
-        own.wait()
-    for lo in range(0, ra, 128):
-        hi = min(lo + 128, ra)
-        block = recv_a[:, :, lo:hi].reshape(n_plane * rows, hi - lo)
-        grads = contract_rows(block, picked_u[...])
-        add_features(grads, m1a[0, lo:hi, :], m2a[0, lo:hi, :], seeds_a[:, lo:hi], hi - lo)
-    for index in range(len(spans)):
-        up_rows(index)
-    summed = block_sums
+            block_sums = add_features(
+                block_sums, grads[lo - low:hi - low], m1b[lo:hi, :], m2b[lo:hi, :], seeds_b[:, lo:hi], hi - lo
+            )
+    summed = [block_sums[:, e * 128:(e + 1) * 128] for e in range(EXAMPLES)]
 
     share = sums.shape[1]
     every = jnp.concatenate(summed, axis=0)

time: 50.3 us -> 50 us (level)
  no operation moved by 1% of the time
where the time goes in v4:
time: 50 us; the launch traced here: 49.8 us
  Pallas kernels  48.5 us (97%)
  local copies, waits for them, and re-layouts  1.28 us (3%)
    pallas_call x1, Pallas kernels, on_device(): pl.pallas_call(functools.partial(kernel, n_ps, n_plane, n_tp, inverse), o...  48.5 us
    unnamed x1, local copies, waits for them, and re-layouts  1.28 us

profile of v4, /device:TPU:0, one launch (start us, length us, event | category | flops | bytes accessed | tf_op | source)
XLA Modules:
  0.0 49.8 jit_solution(10446434406368464583)
XLA Ops:
  0.0 48.5 %shard_map.118 = f32[4,256]{1,0:T(4,128)} custom-call(bf16[128,2048]{1,0:T(8,128)(2,1)} %x_hbm.1, bf16[7392,128]{1,0:T(8,128)(2,1)} %bitcast.4, bf16[2048,128]{1,0:T(8,128)(2,1)} %down_hbm.1, bf16[7392,128]{1,0:T(8,128)(2,1)} %up_hbm.1, f32[1,256,128]{2,1,0:T(8,128)} %m1a_hbm.1, f32[1,256,128]{2,1,0:T(8,128)} %m2a_hbm.1, f32[924,1,128]{2,1,0:T(1,128)} %bitcast.5, ...), custom_call_target="tpu_custom_call" | custom-call | tf_op jit(solution)/shard_map/pallas_call | solution.py:304
  48.5 1.3 %copy.14 = f32[4,256]{1,0:T(4,128)} copy(f32[4,256]{1,0:T(4,128)} %shard_map.118) | data formatting | bytes 8192

commit v5 on v4

--- a/solution.py
+++ b/solution.py
@@ -43,7 +43,7 @@
 
 def pieces_of(rb):
     blocks = -(-rb // 128)
-    ends = [min(rb, 128 * -(-blocks * i // 3)) for i in range(4)]
+    ends = [min(rb, 128 * -(-blocks * i // 4)) for i in range(5)]
     return [(lo, hi) for lo, hi in zip(ends[:-1], ends[1:]) if hi > lo]
 
 

time: 50 us -> 50.1 us (level)
  no operation moved by 1% of the time
where the time goes in v5:
time: 50.1 us; the launch traced here: 49.9 us
  Pallas kernels  48.7 us (97%)
  local copies, waits for them, and re-layouts  1.28 us (3%)
    pallas_call x1, Pallas kernels, on_device(): pl.pallas_call(functools.partial(kernel, n_ps, n_plane, n_tp, inverse), o...  48.7 us
    unnamed x1, local copies, waits for them, and re-layouts  1.28 us

profile of v5, /device:TPU:0, one launch (start us, length us, event | category | flops | bytes accessed | tf_op | source)
XLA Modules:
  0.0 49.9 jit_solution(15206617727532629087)
XLA Ops:
  0.0 48.7 %shard_map.118 = f32[4,256]{1,0:T(4,128)} custom-call(bf16[128,2048]{1,0:T(8,128)(2,1)} %x_hbm.1, bf16[7392,128]{1,0:T(8,128)(2,1)} %bitcast.4, bf16[2048,128]{1,0:T(8,128)(2,1)} %down_hbm.1, bf16[7392,128]{1,0:T(8,128)(2,1)} %up_hbm.1, f32[1,256,128]{2,1,0:T(8,128)} %m1a_hbm.1, f32[1,256,128]{2,1,0:T(8,128)} %m2a_hbm.1, f32[924,1,128]{2,1,0:T(1,128)} %bitcast.5, ...), custom_call_target="tpu_custom_call" | custom-call | tf_op jit(solution)/shard_map/pallas_call | solution.py:304
  48.7 1.3 %copy.14 = f32[4,256]{1,0:T(4,128)} copy(f32[4,256]{1,0:T(4,128)} %shard_map.118) | data formatting | bytes 8192
